TPU v7x, 32 devices: a whole 2x2x4 slice. The times are simulated.
32 devices in a mesh: row: 8 (over z, x), col: 4 (over y, core).
Axes of the slice: x: 2, y: 2, z: 4, core: 2. Of those that a mesh axis runs over, the one named last changes fastest.
Arguments:
- anc_inv: bfloat16 [16384, 16384], P('row', 'col'), may hold values from -0.0546875 to 0.0546875
- panel: bfloat16 [1, 12288, 2048], P(None, 'col', 'row'), may hold values from -6 to 6
- structure: int32 [1, 96], replicated, may hold values from 0 to 127, as said below
Outputs:
- off_inv: float32 [1, 16384, 2048], P(None, 'row', 'col')
Inputs may be any that keep to these rules, and one draw needn't show every extreme that they name: Each structure[s] holds 96 distinct ancestor block indices, in the order in which the panel stores its row blocks (not sorted); each group of 32 consecutive ancestor blocks holds 23 to 25 of them, and some group of each supernode holds exactly 25.
All inputs are finite; a program needn't handle non-finite values.
Results may differ from a plain program's by a relative error of at most 0.0003.
Values may be sent and summed in bfloat16 or wider, within the bound.
A program may use at most 128 MiB of HBM per device.

v0:
```python
import jax
import jax.numpy as jnp
from jax import lax
from jax.sharding import PartitionSpec as P

BS = 128
SBLK = 96


def body(anc_inv, panel, structure):
    col_index = lax.axis_index("col")
    row_index = lax.axis_index("row")
    local_rows, local_cols = anc_inv.shape
    group_blocks = local_cols // BS
    local_width = panel.shape[2]
    gathered = lax.all_gather(panel, "col", axis=1, tiled=True)
    own_blocks = row_index * (local_rows // BS) + jnp.arange(local_rows // BS, dtype=jnp.int32)
    block_ids = jnp.arange(group_blocks, dtype=jnp.int32)
    blocks_of = structure[0]
    compact = gathered[0].reshape(SBLK, BS * local_width)
    local_block = blocks_of - col_index * group_blocks
    picker = (local_block[None, :] == block_ids[:, None]).astype(jnp.bfloat16)
    picked = (
        jnp.dot(picker, compact, preferred_element_type=jnp.float32)
        .astype(jnp.bfloat16)
        .reshape(group_blocks * BS, local_width)
    )
    partial_value = jnp.dot(
        anc_inv,
        lax.all_gather(picked, "row", axis=1, tiled=True),
        preferred_element_type=jnp.float32,
    )
    summed = lax.psum_scatter(partial_value, "col", scatter_dimension=1, tiled=True)
    member = jnp.any(blocks_of[None, :] == own_blocks[:, None], axis=1)
    row_mask = jnp.repeat(member, BS)
    results = [jnp.where(row_mask[:, None], -summed, jnp.zeros_like(summed))]
    return jnp.stack(results)


def solution(mesh):
    in_specs = (P("row", "col"), P(None, "col", "row"), P())
    out_specs = P(None, "row", "col")
    return jax.shard_map(body, mesh=mesh, in_specs=in_specs, out_specs=out_specs, check_vma=False)
```

profile of v0, /device:TPU:7, one launch (start us, length us, event | category | flops | bytes accessed | tf_op | source)
XLA Modules:
  0.0 484.6 jit_solution(2136744149052147059)
XLA Ops:
  6.5 0.0 all-gather.3.cloned.1.call-start
  6.5 0.7 all-gather.3.cloned.1.call-update
  7.3 0.0 all-gather.5.cloned.1.call-start
  7.3 0.7 subtract_bitcast_fusion
  8.0 48.1 %all-gather.3.cloned.1.call-done = bf16[1,12288,256]{2,1,0:T(8,128)(2,1)} async-done(((bf16[1,3072,256]{2,1,0:T(8,128)(2,1)}), bf16[1,12288,256]{2,1,0:T(8,128)(2,1)}) %all-gather.3.cloned.1.call-update) | async-done | bytes 6291472 | tf_op jit(solution)/shard_map/all_gather | solution.py:16
  56.0 10.5 %reshape_squeeze.3 = bf16[96,32768]{1,0:T(8,128)(2,1)} reshape(bf16[1,12288,256]{2,1,0:T(8,128)(2,1)} %all-gather.3.cloned.1.call-done) | data formatting | bytes 12582912 | tf_op jit(solution)/shard_map/reshape;squeeze | solution.py:20
  66.5 3.7 convolution_convert_fusion
  70.2 2.3 reshape.8
  72.6 0.0 all-gather.5.cloned.1.call-update
  72.6 0.0 reduce-scatter.2.cloned.1.call-start
  72.6 228.6 %all-gather.5.cloned.1.call-done = bf16[4096,2048]{1,0:T(8,128)(2,1)} async-done(((bf16[4096,256]{1,0:T(8,128)(2,1)}), bf16[4096,2048]{1,0:T(8,128)(2,1)}) %all-gather.5.cloned.1.call-update) | async-done | bytes 16777232 | tf_op jit(solution)/shard_map/all_gather | solution.py:30
  301.2 43.3 %convolution_bitcast_fusion = f32[2048,2048]{0,1:T(8,128)} fusion(bf16[4096,2048]{1,0:T(8,128)(2,1)} %all-gather.5.cloned.1.call-done, bf16[2048,4096]{1,0:T(8,128)(2,1)} %param.3), kind=kOutput, calls=%fused_computation.1 | convolution fusion | flops 34359738368 | bytes 50331648 | tf_op jit(solution)/shard_map/dot_general | solution.py:28
  344.5 0.0 copy-start
  344.5 0.0 reduce-scatter.2.cloned.1.call-update
  344.5 0.6 copy-done
  345.1 0.2 compare_reduce_fusion
  345.3 0.1 broadcast_bitcast_fusion
  345.4 122.4 %reduce-scatter.2.cloned.1.call-done = f32[2048,512]{0,1:T(8,128)} async-done(((f32[2048,2048]{0,1:T(8,128)}), f32[2048,512]{0,1:T(8,128)}) %reduce-scatter.2.cloned.1.call-update) | async-done | bytes 4194320 | tf_op jit(solution)/shard_map/reduce_scatter | solution.py:33
  467.8 4.9 %select_bitcast_fusion = f32[1,2048,512]{1,2,0:T(8,128)} fusion(f32[2048,512]{0,1:T(8,128)} %reduce-scatter.2.cloned.1.call-done, pred[2048]{0:T(1024)(128)(4,1)S(1)} %broadcast_bitcast_fusion), kind=kLoop, calls=%fused_computation.2 | loop fusion | flops 2097152 | bytes 8390656 | tf_op jit(solution)/shard_map/stack | solution.py:37
  472.8 5.3 %copy.5 = f32[1,2048,512]{2,1,0:T(8,128)} copy(f32[1,2048,512]{1,2,0:T(8,128)} %select_bitcast_fusion) | data formatting | bytes 8388608 | tf_op jit(solution)/shard_map/stack | solution.py:37
  (1 shorter events, 0.0 us)
Async XLA Ops:
  6.5 49.5 %all-gather.3.cloned.1.call-start = ((), (), s32[]{:S(2)}) async-start(), calls=%async_computation.1 | async-start | bytes 7864320 | tf_op jit(solution)/shard_map/all_gather | solution.py:16
  7.3 293.9 %all-gather.5.cloned.1.call-start = ((), (), s32[]{:S(2)}) async-start(), calls=%async_computation.2 | async-start | bytes 18874368 | tf_op jit(solution)/shard_map/all_gather | solution.py:30
  72.6 395.2 %reduce-scatter.2.cloned.1.call-start = ((), (), s32[]{:S(2)}) async-start(), calls=%async_computation.3 | async-start | bytes 20971520 | tf_op jit(solution)/shard_map/reduce_scatter | solution.py:33
  344.5 0.7 copy-start
Sparse Core Ops, SparseCore 0:
  8.9 47.0 all-gather.2
  72.7 228.4 all-gather.4
  344.6 123.1 reduce-scatter.1
where the time goes:
time: 488 us; the launch traced here: 485 us
  waiting for transfers between devices  400 us (82%)
  matrix products  47 us (10%)
  local copies, waits for them, and re-layouts  18.8 us (4%)
  between operations  13.1 us (3%)
  other arithmetic  5.78 us (1%)
    all_gather x1, waiting for transfers between devices, body(): lax.all_gather(picked, 'row', axis=1, tiled=True)  229 us
    reduce_scatter x1, waiting for transfers between devices, body(): lax.psum_scatter(partial_value, 'col', scatter_dimension=1, tiled=True)  122 us
    all_gather x1, waiting for transfers between devices, body(): gathered = lax.all_gather(panel, 'col', axis=1, tiled=True)  48.1 us
    dot_general x1, matrix products, body(): jnp.dot(anc_inv, lax.all_gather(picked, 'row', axis=1, tiled=True), prefe...  43.3 us
    another operation x1, local copies, waits for them, and re-layouts, body(): compact = gathered[0].reshape(SBLK, BS * local_width)  10.5 us
  transfers between devices with their start and end apart: 3, of which 3 were waited for; matrix products, arithmetic and copies ran while one was open for 0% of the time, Pallas kernels for 0%

commit v1 on v0

v1 whole, which is shorter than its diff:
```python
import functools

import jax
import jax.numpy as jnp
from jax import lax
from jax.experimental import pallas as pl
from jax.experimental.pallas import tpu as pltpu
from jax.sharding import PartitionSpec as P

BS = 128
MESH = pl.DeviceIdType.MESH


def kernel(dims, ids, pos, a_hbm, panel_hbm, out_ref,
           G, E, AC, abufs, S, SS, R, RS,
           l_sem, a_sem, g_send, g_recv, e_send, e_recv, r_send, r_recv, rs_send, rs_recv):
    NZ, NX, NC, CAP, H, MB = dims
    NR = NZ * NX
    J = NR // NC
    NCH = NC // 2
    r = lax.axis_index("row")
    c = lax.axis_index("col")
    z, x = r // NX, r % NX
    m, k = c // 2, c % 2
    sibling = m * 2 + 1 - k
    M, K = AC.shape
    w = E.shape[2]
    wh = w // H
    PB = panel_hbm.shape[1]
    GB, RB = abufs[0].shape[:2]
    i32 = lambda v: v.astype(jnp.int32)
    nbrs = [(z + 1 < NZ, r + NX), (z > 0, r - NX), (x + 1 < NX, r + 1), (x > 0, r - 1)]

    def panel_copy(h):
        return pltpu.make_async_copy(
            panel_hbm.at[0, :, :, pl.ds(h * wh, wh)], G[h].at[pl.ds(c * PB, PB)], l_sem.at[h])

    def a_copies(i, b):
        rows = pl.ds(pl.multiple_of(i * RB, RB), RB)
        return [pltpu.make_async_copy(a_hbm.at[rows, pl.ds(q * BS, BS)], abufs[b].at[q], a_sem.at[b, q])
                for q in range(GB)]

    for h in range(H):
        panel_copy(h).start()
    for cp in a_copies(0, 0):
        cp.start()

    barrier = pltpu.get_barrier_semaphore()
    for dc in range(1, NC):
        pl.semaphore_signal(barrier, inc=1, device_id={"col": (c + dc) % NC}, device_id_type=MESH)
    for ok, dev in nbrs:
        @pl.when(ok)
        def _(dev=dev):
            pl.semaphore_signal(barrier, inc=1, device_id={"row": dev}, device_id_type=MESH)
    pl.semaphore_wait(barrier, NC - 1 + sum(i32(ok) for ok, _ in nbrs))

    for h in range(H):
        G[h][NC * PB] = jnp.zeros((BS, wh), jnp.bfloat16)

    def g_copy(h, src, dst, idx):
        blk = G[h].at[pl.ds(src * PB, PB)]
        return pltpu.make_async_remote_copy(
            src_ref=blk, dst_ref=blk, send_sem=g_send.at[h, idx], recv_sem=g_recv.at[h, src],
            device_id={"col": dst}, device_id_type=MESH)

    for h in range(H):
        panel_copy(h).wait()
        for dm in range(1, NCH):
            g_copy(h, c, (m + dm) % NCH * 2 + k, dm - 1).start()
        g_copy(h, c, sibling, NCH - 1).start()

    NA_CH = M // RB

    def pack(p, carry):
        for b in range(2):
            i = p * 2 + b

            @pl.when(i + 1 < NA_CH)
            def _():
                for cp in a_copies(i + 1, 1 - b):
                    cp.start()
            for cp in a_copies(i, b):
                cp.wait()
            rows = pl.ds(pl.multiple_of(i * RB, RB), RB)
            for q in range(CAP):
                AC[rows, q * BS:(q + 1) * BS] = abufs[b][ids[q]]
        return carry

    lax.fori_loop(0, NA_CH // 2, pack, 0)

    def e_copy(j, h, dev, d):
        blk = E.at[j, :, pl.ds(h * wh, wh)]
        return pltpu.make_async_remote_copy(
            src_ref=blk, dst_ref=blk, send_sem=e_send.at[j, h, d], recv_sem=e_recv.at[j, h],
            device_id={"row": dev}, device_id_type=MESH)

    def flags(j):
        zs, xs = j // NX, j % NX
        own = xs == x
        return [own & (zs <= z) & (z + 1 < NZ), own & (zs >= z) & (z > 0),
                (xs <= x) & (x + 1 < NX), (xs >= x) & (x > 0)]

    def forward(j, h, act):
        for d in (2, 3, 0, 1):
            @pl.when(flags(j)[d])
            def _(d=d):
                act(e_copy(j, h, nbrs[d][1], d))

    def slot_of(j):
        return (j - (c + 1) * J + 2 * NR) % NR

    def r_copies(j):
        d, jj = j // J, j % J
        slot = slot_of(j)
        rel = (c - d - 1 + NC) % NC
        return [pltpu.make_async_remote_copy(
            src_ref=a.at[slot], dst_ref=b.at[rel, jj], send_sem=s.at[slot], recv_sem=t.at[rel, jj],
            device_id={"col": d}, device_id_type=MESH)
            for a, b, s, t in ((S, R, r_send, r_recv), (SS, RS, rs_send, rs_recv))]

    def compute(j):
        own = j // J == c
        slot = slot_of(j)

        def chunk(i, carry):
            rows = pl.ds(pl.multiple_of(i * MB, MB), MB)
            prod = jnp.dot(AC[rows, :], E[j], preferred_element_type=jnp.float32)
            for jj in range(J):
                @pl.when(j == c * J + jj)
                def _(jj=jj):
                    out_ref[rows, jj * w:(jj + 1) * w] = prod

            @pl.when(jnp.logical_not(own))
            def _():
                top = jnp.maximum(jnp.max(jnp.abs(prod), axis=0, keepdims=True), 1e-30)
                SS[slot, pl.ds(i, 1), :] = top * (1.0 / 32767.0)
                S[slot, rows, :] = jnp.round(prod * (32767.0 / top)).astype(jnp.int16)
            return carry

        lax.fori_loop(0, M // MB, chunk, 0)

        @pl.when(jnp.logical_not(own))
        def _():
            for cp in r_copies(j):
                cp.start()

    for h in range(H):
        for dm in range(1, NCH):
            src = (m + dm) % NCH * 2 + k
            g_copy(h, src, sibling, 0).wait_recv()
            g_copy(h, src, sibling, NCH - 1 + dm).start()
        for dm in range(NCH):
            g_copy(h, (m + dm) % NCH * 2 + 1 - k, sibling, 0).wait_recv()
        for q in range(CAP):
            E[r, q * BS:(q + 1) * BS, h * wh:(h + 1) * wh] = G[h][pos[q]]
        forward(r, h, lambda cp: cp.start())
    compute(r)

    def zorder(i):
        near = jnp.minimum(z, NZ - 1 - z)
        t = (i + 1) // 2
        two = jnp.where(i % 2 == 1, z - t, z + t)
        one = jnp.where(z < NZ - 1 - z, z + (i - near), z - (i - near))
        return jnp.where(i <= 2 * near, two, one)

    def xorder(i):
        near = jnp.minimum(x, NX - 1 - x)
        t = (i + 1) // 2
        two = jnp.where(i % 2 == 1, x - t, x + t)
        one = jnp.where(x < NX - 1 - x, x + (i - near), x - (i - near))
        return jnp.where(i <= 2 * near, two, one)

    def step(s, carry):
        if NX == 2:
            last = s == 2 * NZ - 1
            d = jnp.where(last, 1, (s + 1) % 2)
            zi = jnp.where(last, NZ - 1, jnp.where(s % 2 == 1, (s + 1) // 2, s // 2 - 1))
            j = zorder(zi) * NX + jnp.where(d == 1, 1 - x, x)
        else:
            j = zorder(s // NX) * NX + xorder(s % NX)
        for h in range(H):
            e_copy(j, h, nbrs[0][1], 0).wait_recv()
            forward(j, h, lambda cp: cp.start())
        compute(j)
        return carry

    lax.fori_loop(1, NR, step, 0)

    for rel in range(NC - 1):
        for jj in range(J):
            for src, dst, s, t in ((S, R, r_send, r_recv), (SS, RS, rs_send, rs_recv)):
                pltpu.make_async_remote_copy(
                    src_ref=src.at[0], dst_ref=dst.at[rel, jj], send_sem=s.at[0], recv_sem=t.at[rel, jj],
                    device_id={"col": sibling}, device_id_type=MESH).wait_recv()
    for jj in range(J):
        def add(i, carry, jj=jj):
            rows = pl.ds(pl.multiple_of(i * MB, MB), MB)
            total = out_ref[rows, jj * w:(jj + 1) * w]
            for rel in range(NC - 1):
                total += R[rel, jj, rows, :].astype(jnp.float32) * RS[rel, jj, pl.ds(i, 1), :]
            out_ref[rows, jj * w:(jj + 1) * w] = total
            return carry
        lax.fori_loop(0, M // MB, add, 0)

    for h in range(H):
        for idx in range(NC - 1):
            g_copy(h, c, sibling, idx).wait_send()

    def drain(j, carry):
        for h in range(H):
            forward(j, h, lambda cp: cp.wait_send())

        @pl.when(j // J != c)
        def _():
            for cp in r_copies(j):
                cp.wait_send()
        return carry

    lax.fori_loop(0, NR, drain, 0)


def body(NR, NC, anc_inv, panel, structure):
    c = lax.axis_index("col")
    r = lax.axis_index("row")
    M, cols = anc_inv.shape
    GB = cols // BS
    CAP = GB * 3 // 4 + 1
    PB, w = panel.shape[1] // BS, panel.shape[2]
    NX = 2
    while NX * NX * 2 < NR:
        NX *= 2
    NZ = NR // NX
    H = max(1, w // 128)
    wh = w // H
    J = NR // NC
    MB = 256
    RB = 256
    K = CAP * BS
    s = structure[0]
    n = s.shape[0]
    at = jnp.arange(n, dtype=jnp.int32)
    mine = s // GB == c
    rank = jnp.sum((at[None, :] < at[:, None]) & mine[None, :], axis=1)
    hot = mine[None, :] & (rank[None, :] == jnp.arange(CAP)[:, None])
    pos = n + jnp.sum(jnp.where(hot, at[None, :] - n, 0), axis=1).astype(jnp.int32)
    ids = jnp.sum(jnp.where(hot, (s - c * GB)[None, :], 0), axis=1).astype(jnp.int32)
    D = pltpu.SemaphoreType.DMA
    chunks = max(8, M // MB)
    smem = pl.BlockSpec(memory_space=pltpu.SMEM)
    hbm = pl.BlockSpec(memory_space=pl.ANY)
    total = pl.pallas_call(
        functools.partial(kernel, (NZ, NX, NC, CAP, H, MB)),
        out_shape=jax.ShapeDtypeStruct((M, J * w), jnp.float32),
        in_specs=[smem, smem, hbm, hbm],
        out_specs=pl.BlockSpec(memory_space=pltpu.VMEM),
        scratch_shapes=[
            [pltpu.VMEM((NC * PB + 1, BS, wh), jnp.bfloat16)] * H,
            pltpu.VMEM((NR, K, w), jnp.bfloat16),
            pltpu.VMEM((M, K), jnp.bfloat16),
            [pltpu.VMEM((GB, RB, BS), jnp.bfloat16)] * 2,
            pltpu.VMEM((NR - J, M, w), jnp.int16),
            pltpu.VMEM((NR - J, chunks, w), jnp.float32),
            pltpu.VMEM((NC - 1, J, M, w), jnp.int16),
            pltpu.VMEM((NC - 1, J, chunks, w), jnp.float32),
            D((H,)), D((2, GB)), D((H, NC - 1)), D((H, NC)), D((NR, H, 4)), D((NR, H)),
            D((NR - J,)), D((NC - 1, J)), D((NR - J,)), D((NC - 1, J)),
        ],
        compiler_params=pltpu.CompilerParams(
            collective_id=0, has_side_effects=True, vmem_limit_bytes=63 * 2**20),
    )(ids, pos, anc_inv, panel.reshape(1, PB, BS, w))
    own_blocks = r * (M // BS) + jnp.arange(M // BS, dtype=jnp.int32)
    member = jnp.any(s[None, :] == own_blocks[:, None], axis=1)
    mask = jnp.repeat(member, BS)
    return jnp.where(mask[:, None], -total, 0.0)[None]


def solution(mesh):
    in_specs = (P("row", "col"), P(None, "col", "row"), P())
    out_specs = P(None, "row", "col")
    fn = functools.partial(body, mesh.shape["row"], mesh.shape["col"])
    return jax.shard_map(fn, mesh=mesh, in_specs=in_specs, out_specs=out_specs, check_vma=False)
```

time: 488 us -> 231 us (0.47)
  waiting for transfers between devices: 400 us -> 0 us
  Pallas kernels: 0 us -> 224 us
  matrix products: 47 us -> 0 us
  local copies, waits for them, and re-layouts: 18.8 us -> 0.08 us
  between operations: 13.1 us -> 0.04 us
    all_gather x2 -> x0, waiting for transfers between devices: 277 us -> none  [the longest x1 229 us: body(): lax.all_gather(picked, 'row', axis=1, tiled=True)]
    pallas_call x0 -> x1, Pallas kernels: none -> 224 us  [body(): pl.pallas_call(functools.partial(kernel, (NZ, NX, NC, CAP, H, MB)), out_s...]
    reduce_scatter x1 -> x0, waiting for transfers between devices: 122 us -> none  [body(): lax.psum_scatter(partial_value, 'col', scatter_dimension=1, tiled=True)]
    dot_general x2 -> x0, matrix products: 47 us -> none  [the longest x1 43.3 us: body(): jnp.dot(anc_inv, lax.all_gather(picked, 'row', axis=1, tiled=True), prefe...]
    another operation x2 -> x0, local copies, waits for them, and re-layouts: 15.8 us -> none  [the longest x1 10.5 us: body(): compact = gathered[0].reshape(SBLK, BS * local_width)]
    another operation x1 -> x0, other arithmetic: 4.93 us -> none  [body(): return jnp.stack(results)]
  transfers between devices with their start and end apart: 3 -> 0, of which waited for: 3 -> 0; matrix products, arithmetic and copies ran while one was open for 0% -> 0% of each run, Pallas kernels for 0% -> 0%
where the time goes in v1:
time: 231 us
  Pallas kernels  224 us (97%)
  other arithmetic  6.67 us (3%)
    pallas_call x1, Pallas kernels, body(): pl.pallas_call(functools.partial(kernel, (NZ, NX, NC, CAP, H, MB)), out_s...  224 us

profile of v1, /device:TPU:7, one launch (start us, length us, event | category | flops | bytes accessed | tf_op | source)
XLA Modules:
  0.0 230.8 jit_solution(6868924899274231901)
XLA Ops:
  0.0 0.7 compare_bitcast_fusion
  0.7 0.1 convert_reduce_fusion
  0.8 0.7 subtract_bitcast_fusion
  1.4 0.6 select_reduce_fusion
  2.1 0.5 broadcast_add_fusion.pos
  2.6 0.0 copy-start
  2.6 224.1 %shard_map.37 = f32[2048,512]{1,0:T(8,128)} custom-call(s32[25]{0:T(128)} %get-tuple-element.6.ids, s32[25]{0:T(128)} %broadcast_add_fusion.pos, bf16[2048,4096]{1,0:T(8,128)(2,1)} %a_hbm.1, bf16[1,24,128,256]{3,2,1,0:T(8,128)(2,1)} %bitcast.10), custom_call_target="tpu_custom_call" | custom-call | tf_op jit(solution)/shard_map/pallas_call | solution.py:251
  226.7 0.0 copy-done
  226.7 0.2 compare_reduce_fusion
  226.9 0.1 broadcast_bitcast_fusion
  227.0 3.9 %select_bitcast_fusion = f32[1,2048,512]{2,1,0:T(8,128)} fusion(f32[2048,512]{1,0:T(8,128)} %shard_map.37, pred[2048]{0:T(1024)(128)(4,1)S(1)} %broadcast_bitcast_fusion), kind=kLoop, calls=%fused_computation | loop fusion | flops 2097152 | bytes 8390656 | tf_op jit(solution)/shard_map/broadcast_in_dim | solution.py:274
  (2 shorter events, 0.0 us)
Async XLA Ops:
  2.6 224.1 %copy-start = (s32[1,96]{1,0:T(1,128)S(1)}, s32[1,96]{1,0:T(1,128)}, u32[]{:S(2)}) copy-start(s32[1,96]{1,0:T(1,128)} %param.5) | copy-start | bytes 1156

commit v2 on v1

--- a/solution.py
+++ b/solution.py
@@ -12,9 +12,9 @@
 
 
 def kernel(dims, ids, pos, a_hbm, panel_hbm, out_ref,
-           G, E, AC, abufs, S, SS, R, RS,
-           l_sem, a_sem, g_send, g_recv, e_send, e_recv, r_send, r_recv, rs_send, rs_recv):
-    NZ, NX, NC, CAP, H, MB = dims
+           G, E, AC, abufs, Y, far_bufs, mate_bufs, half_bufs,
+           l_sem, a_sem, g_send, g_recv, e_send, e_recv, far_sems, mate_sems, half_sems):
+    NZ, NX, NC, CAP, H, MB, MM, KA = dims
     NR = NZ * NX
     J = NR // NC
     NCH = NC // 2
@@ -24,6 +24,7 @@
     m, k = c // 2, c % 2
     sibling = m * 2 + 1 - k
     M, K = AC.shape
+    HM = M // 2
     w = E.shape[2]
     wh = w // H
     PB = panel_hbm.shape[1]
@@ -88,60 +89,110 @@
 
     lax.fori_loop(0, NA_CH // 2, pack, 0)
 
-    def e_copy(j, h, dev, d):
-        blk = E.at[j, :, pl.ds(h * wh, wh)]
+    PARTS = ((1, KA, K - KA), (0, 0, KA))
+
+    def e_copy(j, h, part, dev, d):
+        p, first, count = part
+        blk = E.at[j, pl.ds(first, count), pl.ds(h * wh, wh)]
         return pltpu.make_async_remote_copy(
-            src_ref=blk, dst_ref=blk, send_sem=e_send.at[j, h, d], recv_sem=e_recv.at[j, h],
+            src_ref=blk, dst_ref=blk, send_sem=e_send.at[j, h, p, d], recv_sem=e_recv.at[j, h, p],
             device_id={"row": dev}, device_id_type=MESH)
 
-    def flags(j):
+    def flags(j, p):
         zs, xs = j // NX, j % NX
-        own = xs == x
-        return [own & (zs <= z) & (z + 1 < NZ), own & (zs >= z) & (z > 0),
-                (xs <= x) & (x + 1 < NX), (xs >= x) & (x > 0)]
-
-    def forward(j, h, act):
+        along_z = (xs == x) | (p == 1)
+        along_x = (zs == z) | (p == 0)
+        return [along_z & (zs <= z) & (z + 1 < NZ), along_z & (zs >= z) & (z > 0),
+                along_x & (xs <= x) & (x + 1 < NX), along_x & (xs >= x) & (x > 0)]
+
+    def forward(j, h, part, act):
         for d in (2, 3, 0, 1):
-            @pl.when(flags(j)[d])
+            @pl.when(flags(j, part[0])[d])
             def _(d=d):
-                act(e_copy(j, h, nbrs[d][1], d))
-
-    def slot_of(j):
-        return (j - (c + 1) * J + 2 * NR) % NR
-
-    def r_copies(j):
-        d, jj = j // J, j % J
-        slot = slot_of(j)
-        rel = (c - d - 1 + NC) % NC
+                act(e_copy(j, h, part, nbrs[d][1], d))
+
+    def pair(bufs, sems, src, dst, i, j, dev):
         return [pltpu.make_async_remote_copy(
-            src_ref=a.at[slot], dst_ref=b.at[rel, jj], send_sem=s.at[slot], recv_sem=t.at[rel, jj],
-            device_id={"col": d}, device_id_type=MESH)
-            for a, b, s, t in ((S, R, r_send, r_recv), (SS, RS, rs_send, rs_recv))]
+            src_ref=bufs[q].at[src], dst_ref=bufs[q + 2].at[dst], send_sem=sems[q].at[i], recv_sem=sems[q + 2].at[j],
+            device_id={"col": dev}, device_id_type=MESH) for q in range(2)]
+
+    def far_slot(j):
+        return (j - (m + 1) * 2 * J + 2 * NR) % NR
+
+    def half_copies(slot):
+        return pair(half_bufs, half_sems, slot, slot, slot, slot, sibling)
+
+    def mate_copies(jj):
+        return pair(mate_bufs, mate_sems, jj, jj, jj, jj, sibling)
+
+    def far_copies(j):
+        slot, md = far_slot(j), j // (2 * J)
+        at = ((m - md - 1 + NCH) % NCH, j % J, k)
+        return pair(far_bufs, far_sems, slot, at, slot, at, j // J)
+
+    def encode(value, dst, scales, slot, row0, i):
+        top = jnp.maximum(jnp.max(jnp.abs(value), axis=0, keepdims=True), 1e-30)
+        scales[slot, pl.ds(i, 1), :] = top * (1.0 / 32767.0)
+        dst[slot, pl.ds(pl.multiple_of(row0, MB), MB), :] = jnp.round(value * (32767.0 / top)).astype(jnp.int16)
 
     def compute(j):
-        own = j // J == c
-        slot = slot_of(j)
-
-        def chunk(i, carry):
-            rows = pl.ds(pl.multiple_of(i * MB, MB), MB)
-            prod = jnp.dot(AC[rows, :], E[j], preferred_element_type=jnp.float32)
-            for jj in range(J):
-                @pl.when(j == c * J + jj)
-                def _(jj=jj):
-                    out_ref[rows, jj * w:(jj + 1) * w] = prod
-
-            @pl.when(jnp.logical_not(own))
-            def _():
-                top = jnp.maximum(jnp.max(jnp.abs(prod), axis=0, keepdims=True), 1e-30)
-                SS[slot, pl.ds(i, 1), :] = top * (1.0 / 32767.0)
-                S[slot, rows, :] = jnp.round(prod * (32767.0 / top)).astype(jnp.int16)
-            return carry
-
-        lax.fori_loop(0, M // MB, chunk, 0)
-
-        @pl.when(jnp.logical_not(own))
+        jj, d = j % J, j // J
+        far = d // 2 != m
+        slot = far_slot(j)
+
+        def rows_of(half, keep):
+            def chunk(i, carry):
+                row0 = half * HM + i * MM
+                prod = jnp.dot(AC[pl.ds(pl.multiple_of(row0, MM), MM), :], E[j], preferred_element_type=jnp.float32)
+                for o in range(J):
+                    @pl.when(j == c * J + o)
+                    def _(o=o):
+                        out_ref[pl.ds(pl.multiple_of(row0, MM), MM), o * w:(o + 1) * w] = prod
+
+                @pl.when(d == sibling)
+                def _():
+                    for u in range(MM // MB):
+                        encode(prod[u * MB:(u + 1) * MB], mate_bufs[0], mate_bufs[1], jj, row0 + u * MB, row0 // MB + u)
+
+                @pl.when(far)
+                def _():
+                    if keep:
+                        Y[pl.ds(pl.multiple_of(i * MM, MM), MM), :] = prod
+                    else:
+                        for u in range(MM // MB):
+                            encode(prod[u * MB:(u + 1) * MB], half_bufs[0], half_bufs[1], slot,
+                                   i * MM + u * MB, i * (MM // MB) + u)
+                return carry
+
+            lax.fori_loop(0, HM // MM, chunk, 0)
+
+        rows_of(1 - k, False)
+
+        @pl.when(far)
         def _():
-            for cp in r_copies(j):
+            for cp in half_copies(slot):
+                cp.start()
+
+        rows_of(k, True)
+
+        @pl.when(d == sibling)
+        def _():
+            for cp in mate_copies(jj):
+                cp.start()
+
+        @pl.when(far)
+        def _():
+            for cp in half_copies(slot):
+                cp.wait_recv()
+
+            def chunk(i, carry):
+                rows = pl.ds(pl.multiple_of(i * MB, MB), MB)
+                value = Y[rows, :] + half_bufs[2][slot, rows, :].astype(jnp.float32) * half_bufs[3][slot, pl.ds(i, 1), :]
+                encode(value, far_bufs[0], far_bufs[1], slot, i * MB, i)
+                return carry
+
+            lax.fori_loop(0, HM // MB, chunk, 0)
+            for cp in far_copies(j):
                 cp.start()
 
     for h in range(H):
@@ -153,7 +204,8 @@
             g_copy(h, (m + dm) % NCH * 2 + 1 - k, sibling, 0).wait_recv()
         for q in range(CAP):
             E[r, q * BS:(q + 1) * BS, h * wh:(h + 1) * wh] = G[h][pos[q]]
-        forward(r, h, lambda cp: cp.start())
+        for part in PARTS:
+            forward(r, h, part, lambda cp: cp.start())
     compute(r)
 
     def zorder(i):
@@ -179,25 +231,31 @@
         else:
             j = zorder(s // NX) * NX + xorder(s % NX)
         for h in range(H):
-            e_copy(j, h, nbrs[0][1], 0).wait_recv()
-            forward(j, h, lambda cp: cp.start())
+            for part in PARTS:
+                e_copy(j, h, part, nbrs[0][1], 0).wait_recv()
+                forward(j, h, part, lambda cp: cp.start())
         compute(j)
         return carry
 
     lax.fori_loop(1, NR, step, 0)
 
-    for rel in range(NC - 1):
-        for jj in range(J):
-            for src, dst, s, t in ((S, R, r_send, r_recv), (SS, RS, rs_send, rs_recv)):
-                pltpu.make_async_remote_copy(
-                    src_ref=src.at[0], dst_ref=dst.at[rel, jj], send_sem=s.at[0], recv_sem=t.at[rel, jj],
-                    device_id={"col": sibling}, device_id_type=MESH).wait_recv()
     for jj in range(J):
+        for cp in mate_copies(jj):
+            cp.wait_recv()
+        for rel in range(NCH - 1):
+            for half in range(2):
+                for cp in pair(far_bufs, far_sems, 0, (rel, jj, half), 0, (rel, jj, half), sibling):
+                    cp.wait_recv()
+
         def add(i, carry, jj=jj):
             rows = pl.ds(pl.multiple_of(i * MB, MB), MB)
+            half, ih = i // (HM // MB), i % (HM // MB)
+            inner = pl.ds(pl.multiple_of(ih * MB, MB), MB)
             total = out_ref[rows, jj * w:(jj + 1) * w]
-            for rel in range(NC - 1):
-                total += R[rel, jj, rows, :].astype(jnp.float32) * RS[rel, jj, pl.ds(i, 1), :]
+            total += mate_bufs[2][jj, rows, :].astype(jnp.float32) * mate_bufs[3][jj, pl.ds(i, 1), :]
+            for rel in range(NCH - 1):
+                total += (far_bufs[2][rel, jj, half, inner, :].astype(jnp.float32)
+                          * far_bufs[3][rel, jj, half, pl.ds(ih, 1), :])
             out_ref[rows, jj * w:(jj + 1) * w] = total
             return carry
         lax.fori_loop(0, M // MB, add, 0)
@@ -208,14 +266,18 @@
 
     def drain(j, carry):
         for h in range(H):
-            forward(j, h, lambda cp: cp.wait_send())
-
-        @pl.when(j // J != c)
+            for part in PARTS:
+                forward(j, h, part, lambda cp: cp.wait_send())
+
+        @pl.when(j // (2 * J) != m)
         def _():
-            for cp in r_copies(j):
+            for cp in half_copies(far_slot(j)) + far_copies(j):
                 cp.wait_send()
         return carry
 
+    for jj in range(J):
+        for cp in mate_copies(jj):
+            cp.wait_send()
     lax.fori_loop(0, NR, drain, 0)
 
 
@@ -233,9 +295,12 @@
     H = max(1, w // 128)
     wh = w // H
     J = NR // NC
+    HM = M // 2
     MB = 256
+    MM = min(512, HM)
     RB = 256
     K = CAP * BS
+    KA = (CAP - (CAP + 3) // 6) * BS
     s = structure[0]
     n = s.shape[0]
     at = jnp.arange(n, dtype=jnp.int32)
@@ -245,11 +310,21 @@
     pos = n + jnp.sum(jnp.where(hot, at[None, :] - n, 0), axis=1).astype(jnp.int32)
     ids = jnp.sum(jnp.where(hot, (s - c * GB)[None, :], 0), axis=1).astype(jnp.int32)
     D = pltpu.SemaphoreType.DMA
-    chunks = max(8, M // MB)
+    far = NR - 2 * J
+    lead = (NC // 2 - 1, J, 2)
+
+    def bufs(send, recv, rows):
+        chunks = max(8, rows // MB)
+        return [pltpu.VMEM((*send, rows, w), jnp.int16), pltpu.VMEM((*send, chunks, w), jnp.float32),
+                pltpu.VMEM((*recv, rows, w), jnp.int16), pltpu.VMEM((*recv, chunks, w), jnp.float32)]
+
+    def sems(send, recv):
+        return [D(send), D(send), D(recv), D(recv)]
+
     smem = pl.BlockSpec(memory_space=pltpu.SMEM)
     hbm = pl.BlockSpec(memory_space=pl.ANY)
     total = pl.pallas_call(
-        functools.partial(kernel, (NZ, NX, NC, CAP, H, MB)),
+        functools.partial(kernel, (NZ, NX, NC, CAP, H, MB, MM, KA)),
         out_shape=jax.ShapeDtypeStruct((M, J * w), jnp.float32),
         in_specs=[smem, smem, hbm, hbm],
         out_specs=pl.BlockSpec(memory_space=pltpu.VMEM),
@@ -258,12 +333,10 @@
             pltpu.VMEM((NR, K, w), jnp.bfloat16),
             pltpu.VMEM((M, K), jnp.bfloat16),
             [pltpu.VMEM((GB, RB, BS), jnp.bfloat16)] * 2,
-            pltpu.VMEM((NR - J, M, w), jnp.int16),
-            pltpu.VMEM((NR - J, chunks, w), jnp.float32),
-            pltpu.VMEM((NC - 1, J, M, w), jnp.int16),
-            pltpu.VMEM((NC - 1, J, chunks, w), jnp.float32),
-            D((H,)), D((2, GB)), D((H, NC - 1)), D((H, NC)), D((NR, H, 4)), D((NR, H)),
-            D((NR - J,)), D((NC - 1, J)), D((NR - J,)), D((NC - 1, J)),
+            pltpu.VMEM((HM, w), jnp.float32),
+            bufs((far,), lead, HM), bufs((J,), (J,), M), bufs((far,), (far,), HM),
+            D((H,)), D((2, GB)), D((H, NC - 1)), D((H, NC)), D((NR, H, 2, 4)), D((NR, H, 2)),
+            sems((far,), lead), sems((J,), (J,)), sems((far,), (far,)),
         ],
         compiler_params=pltpu.CompilerParams(
             collective_id=0, has_side_effects=True, vmem_limit_bytes=63 * 2**20),

time: 231 us -> 197 us (0.85)
  Pallas kernels: 224 us -> 190 us
    pallas_call x1, Pallas kernels: 224 us -> 190 us  [body(): pl.pallas_call(functools.partial(kernel, (NZ, NX, NC, CAP, H, MB, MM, KA)...]
where the time goes in v2:
time: 197 us
  Pallas kernels  190 us (96%)
  other arithmetic  6.67 us (3%)
    pallas_call x1, Pallas kernels, body(): pl.pallas_call(functools.partial(kernel, (NZ, NX, NC, CAP, H, MB, MM, KA)...  190 us

profile of v2, /device:TPU:7, one launch (start us, length us, event | category | flops | bytes accessed | tf_op | source)
XLA Modules:
  0.0 196.8 jit_solution(5272532696351046904)
XLA Ops:
  0.0 0.7 compare_bitcast_fusion
  0.7 0.1 convert_reduce_fusion
  0.8 0.7 subtract_bitcast_fusion
  1.4 0.6 select_reduce_fusion
  2.1 0.5 broadcast_add_fusion.pos
  2.6 0.0 copy-start
  2.6 190.0 %shard_map.37 = f32[2048,512]{1,0:T(8,128)} custom-call(s32[25]{0:T(128)} %get-tuple-element.6.ids, s32[25]{0:T(128)} %broadcast_add_fusion.pos, bf16[2048,4096]{1,0:T(8,128)(2,1)} %a_hbm.1, bf16[1,24,128,256]{3,2,1,0:T(8,128)(2,1)} %bitcast.10), custom_call_target="tpu_custom_call" | custom-call | tf_op jit(solution)/shard_map/pallas_call | solution.py:326
  192.6 0.0 copy-done
  192.6 0.2 compare_reduce_fusion
  192.8 0.1 broadcast_bitcast_fusion
  192.9 3.9 %select_bitcast_fusion = f32[1,2048,512]{2,1,0:T(8,128)} fusion(f32[2048,512]{1,0:T(8,128)} %shard_map.37, pred[2048]{0:T(1024)(128)(4,1)S(1)} %broadcast_bitcast_fusion), kind=kLoop, calls=%fused_computation | loop fusion | flops 2097152 | bytes 8390656 | tf_op jit(solution)/shard_map/broadcast_in_dim | solution.py:347
  (2 shorter events, 0.0 us)
Async XLA Ops:
  2.6 190.0 %copy-start = (s32[1,96]{1,0:T(1,128)S(1)}, s32[1,96]{1,0:T(1,128)}, u32[]{:S(2)}) copy-start(s32[1,96]{1,0:T(1,128)} %param.5) | copy-start | bytes 1156

commit v3 on v2

--- a/solution.py
+++ b/solution.py
@@ -111,88 +111,87 @@
             def _(d=d):
                 act(e_copy(j, h, part, nbrs[d][1], d))
 
-    def pair(bufs, sems, src, dst, i, j, dev):
+    def pair(bufs, sems, src, dst, i, j, dev, lo=0, n=None):
+        lanes = (slice(None),) * (len(bufs[0].shape) - 1 - len(src)) + (pl.ds(lo, n or w),)
         return [pltpu.make_async_remote_copy(
-            src_ref=bufs[q].at[src], dst_ref=bufs[q + 2].at[dst], send_sem=sems[q].at[i], recv_sem=sems[q + 2].at[j],
+            src_ref=bufs[q].at[(*src, *lanes)], dst_ref=bufs[q + 2].at[(*dst, *lanes)],
+            send_sem=sems[q].at[i], recv_sem=sems[q + 2].at[j],
             device_id={"col": dev}, device_id_type=MESH) for q in range(2)]
 
     def far_slot(j):
         return (j - (m + 1) * 2 * J + 2 * NR) % NR
 
-    def half_copies(slot):
-        return pair(half_bufs, half_sems, slot, slot, slot, slot, sibling)
-
-    def mate_copies(jj):
-        return pair(mate_bufs, mate_sems, jj, jj, jj, jj, sibling)
-
-    def far_copies(j):
+    def half_copies(slot, lo=0, n=None):
+        return pair(half_bufs, half_sems, (slot,), (slot,), slot, (slot, int(lo > 0)), sibling, lo, n)
+
+    def mate_copies(jj, lo=0, n=None):
+        return pair(mate_bufs, mate_sems, (jj,), (jj,), jj, jj, sibling, lo, n)
+
+    def far_copies(j, lo=0, n=None):
         slot, md = far_slot(j), j // (2 * J)
         at = ((m - md - 1 + NCH) % NCH, j % J, k)
-        return pair(far_bufs, far_sems, slot, at, slot, at, j // J)
-
-    def encode(value, dst, scales, slot, row0, i):
+        return pair(far_bufs, far_sems, (slot,), at, slot, at, j // J, lo, n)
+
+    def encode(value, bufs, slot, i, lo, n):
         top = jnp.maximum(jnp.max(jnp.abs(value), axis=0, keepdims=True), 1e-30)
-        scales[slot, pl.ds(i, 1), :] = top * (1.0 / 32767.0)
-        dst[slot, pl.ds(pl.multiple_of(row0, MB), MB), :] = jnp.round(value * (32767.0 / top)).astype(jnp.int16)
-
-    def compute(j):
+        bufs[1][*slot, i:i + 1, lo:lo + n] = top * (1.0 / 32767.0)
+        bufs[0][*slot, i * MB:(i + 1) * MB, lo:lo + n] = jnp.round(
+            value * (32767.0 / top)).astype(jnp.int16)
+
+    def product(j, half, keep, lo, n):
         jj, d = j % J, j // J
-        far = d // 2 != m
         slot = far_slot(j)
 
-        def rows_of(half, keep):
-            def chunk(i, carry):
-                row0 = half * HM + i * MM
-                prod = jnp.dot(AC[pl.ds(pl.multiple_of(row0, MM), MM), :], E[j], preferred_element_type=jnp.float32)
-                for o in range(J):
-                    @pl.when(j == c * J + o)
-                    def _(o=o):
-                        out_ref[pl.ds(pl.multiple_of(row0, MM), MM), o * w:(o + 1) * w] = prod
-
-                @pl.when(d == sibling)
-                def _():
-                    for u in range(MM // MB):
-                        encode(prod[u * MB:(u + 1) * MB], mate_bufs[0], mate_bufs[1], jj, row0 + u * MB, row0 // MB + u)
-
-                @pl.when(far)
-                def _():
-                    if keep:
-                        Y[pl.ds(pl.multiple_of(i * MM, MM), MM), :] = prod
-                    else:
-                        for u in range(MM // MB):
-                            encode(prod[u * MB:(u + 1) * MB], half_bufs[0], half_bufs[1], slot,
-                                   i * MM + u * MB, i * (MM // MB) + u)
-                return carry
-
-            lax.fori_loop(0, HM // MM, chunk, 0)
-
-        rows_of(1 - k, False)
-
-        @pl.when(far)
+        for i in range(HM // MM):
+            rows = pl.ds(pl.multiple_of(half * HM + i * MM, MM), MM)
+            prod = jnp.dot(AC[rows, :], E[j, :, lo:lo + n], preferred_element_type=jnp.float32)
+            parts = [(i * (MM // MB) + u, prod[u * MB:(u + 1) * MB]) for u in range(MM // MB)]
+            for o in range(J):
+                @pl.when(j == c * J + o)
+                def _(o=o):
+                    out_ref[rows, o * w + lo:o * w + lo + n] = prod
+
+            @pl.when(d == sibling)
+            def _():
+                for u, part in parts:
+                    encode(part, mate_bufs, (jj, half), u, lo, n)
+
+            @pl.when(d // 2 != m)
+            def _():
+                if keep:
+                    Y[i * MM:(i + 1) * MM, lo:lo + n] = prod
+                else:
+                    for u, part in parts:
+                        encode(part, half_bufs, (slot,), u, lo, n)
+
+    def first_half(j, lo, n):
+        product(j, 1 - k, False, lo, n)
+
+        @pl.when(j // (2 * J) != m)
         def _():
-            for cp in half_copies(slot):
+            for cp in half_copies(far_slot(j), lo, n):
                 cp.start()
 
-        rows_of(k, True)
-
-        @pl.when(d == sibling)
+    def second_half(j, lo, n):
+        product(j, k, True, lo, n)
+        slot = far_slot(j)
+
+        @pl.when(j // J == sibling)
         def _():
-            for cp in mate_copies(jj):
+            for cp in mate_copies(j % J, lo, n):
                 cp.start()
 
-        @pl.when(far)
+        @pl.when(j // (2 * J) != m)
         def _():
-            for cp in half_copies(slot):
+            for cp in half_copies(slot, lo, n):
                 cp.wait_recv()
 
-            def chunk(i, carry):
-                rows = pl.ds(pl.multiple_of(i * MB, MB), MB)
-                value = Y[rows, :] + half_bufs[2][slot, rows, :].astype(jnp.float32) * half_bufs[3][slot, pl.ds(i, 1), :]
-                encode(value, far_bufs[0], far_bufs[1], slot, i * MB, i)
-                return carry
-
-            lax.fori_loop(0, HM // MB, chunk, 0)
-            for cp in far_copies(j):
+            for i in range(HM // MB):
+                rows = slice(i * MB, (i + 1) * MB)
+                other = half_bufs[2][slot, rows, lo:lo + n].astype(jnp.float32)
+                value = Y[rows, lo:lo + n] + other * half_bufs[3][slot, i:i + 1, lo:lo + n]
+                encode(value, far_bufs, (slot,), i, lo, n)
+            for cp in far_copies(j, lo, n):
                 cp.start()
 
     for h in range(H):
@@ -206,7 +205,6 @@
             E[r, q * BS:(q + 1) * BS, h * wh:(h + 1) * wh] = G[h][pos[q]]
         for part in PARTS:
             forward(r, h, part, lambda cp: cp.start())
-    compute(r)
 
     def zorder(i):
         near = jnp.minimum(z, NZ - 1 - z)
@@ -222,29 +220,46 @@
         one = jnp.where(x < NX - 1 - x, x + (i - near), x - (i - near))
         return jnp.where(i <= 2 * near, two, one)
 
+    def slice_at(s):
+        if NX != 2:
+            return zorder(s // NX) * NX + xorder(s % NX)
+        lead = jnp.where((z > 0) & (z + 1 < NZ), min(2, NZ - 1), 1)
+        u = s - lead - 1
+        both = 2 * (NZ - 1 - lead)
+        z_turn = (s <= lead) | ((u < both) & (u % 2 == 1))
+        zi = jnp.where(s <= lead, s, jnp.where(u < both, jnp.where(u % 2 == 1, lead + 1 + u // 2, u // 2), u - both // 2))
+        return zorder(zi) * NX + jnp.where(z_turn, x, 1 - x)
+
+    def arrive(j, h):
+        for part in PARTS:
+            e_copy(j, h, part, nbrs[0][1], 0).wait_recv()
+            forward(j, h, part, lambda cp: cp.start())
+
     def step(s, carry):
-        if NX == 2:
-            last = s == 2 * NZ - 1
-            d = jnp.where(last, 1, (s + 1) % 2)
-            zi = jnp.where(last, NZ - 1, jnp.where(s % 2 == 1, (s + 1) // 2, s // 2 - 1))
-            j = zorder(zi) * NX + jnp.where(d == 1, 1 - x, x)
-        else:
-            j = zorder(s // NX) * NX + xorder(s % NX)
+        j, before = slice_at(s), slice_at(s - 1)
+        first_half(before, 0, w)
         for h in range(H):
-            for part in PARTS:
-                e_copy(j, h, part, nbrs[0][1], 0).wait_recv()
-                forward(j, h, part, lambda cp: cp.start())
-        compute(j)
+            arrive(j, h)
+            if h == 0:
+                second_half(before, 0, w)
         return carry
 
-    lax.fori_loop(1, NR, step, 0)
+    lax.fori_loop(1, NR - 1, step, 0)
+    last, before = slice_at(jnp.int32(NR - 1)), slice_at(jnp.int32(NR - 2))
+    first_half(before, 0, w)
+    for h in range(H):
+        arrive(last, h)
+        if h == 0:
+            second_half(before, 0, w)
+        first_half(last, h * wh, wh)
+        second_half(last, h * wh, wh)
 
     for jj in range(J):
         for cp in mate_copies(jj):
             cp.wait_recv()
         for rel in range(NCH - 1):
             for half in range(2):
-                for cp in pair(far_bufs, far_sems, 0, (rel, jj, half), 0, (rel, jj, half), sibling):
+                for cp in pair(far_bufs, far_sems, (0,), (rel, jj, half), 0, (rel, jj, half), sibling):
                     cp.wait_recv()
 
         def add(i, carry, jj=jj):
@@ -252,7 +267,7 @@
             half, ih = i // (HM // MB), i % (HM // MB)
             inner = pl.ds(pl.multiple_of(ih * MB, MB), MB)
             total = out_ref[rows, jj * w:(jj + 1) * w]
-            total += mate_bufs[2][jj, rows, :].astype(jnp.float32) * mate_bufs[3][jj, pl.ds(i, 1), :]
+            total += mate_bufs[2][jj, half, inner, :].astype(jnp.float32) * mate_bufs[3][jj, half, pl.ds(ih, 1), :]
             for rel in range(NCH - 1):
                 total += (far_bufs[2][rel, jj, half, inner, :].astype(jnp.float32)
                           * far_bufs[3][rel, jj, half, pl.ds(ih, 1), :])
@@ -334,9 +349,9 @@
             pltpu.VMEM((M, K), jnp.bfloat16),
             [pltpu.VMEM((GB, RB, BS), jnp.bfloat16)] * 2,
             pltpu.VMEM((HM, w), jnp.float32),
-            bufs((far,), lead, HM), bufs((J,), (J,), M), bufs((far,), (far,), HM),
+            bufs((far,), lead, HM), bufs((J, 2), (J, 2), HM), bufs((far,), (far,), HM),
             D((H,)), D((2, GB)), D((H, NC - 1)), D((H, NC)), D((NR, H, 2, 4)), D((NR, H, 2)),
-            sems((far,), lead), sems((J,), (J,)), sems((far,), (far,)),
+            sems((far,), lead), sems((J,), (J,)), sems((far,), (far, 2)),
         ],
         compiler_params=pltpu.CompilerParams(
             collective_id=0, has_side_effects=True, vmem_limit_bytes=63 * 2**20),

time: 197 us -> 200 us (1.015)
  Pallas kernels: 190 us -> 193 us
    pallas_call x1, Pallas kernels: 190 us -> 193 us  [body(): pl.pallas_call(functools.partial(kernel, (NZ, NX, NC, CAP, H, MB, MM, KA)...]
where the time goes in v3:
time: 200 us
  Pallas kernels  193 us (96%)
  other arithmetic  6.67 us (3%)
    pallas_call x1, Pallas kernels, body(): pl.pallas_call(functools.partial(kernel, (NZ, NX, NC, CAP, H, MB, MM, KA)...  193 us

profile of v3, /device:TPU:7, one launch (start us, length us, event | category | flops | bytes accessed | tf_op | source)
XLA Modules:
  0.0 199.8 jit_solution(12502599479702923299)
XLA Ops:
  0.0 0.7 compare_bitcast_fusion
  0.7 0.1 convert_reduce_fusion
  0.8 0.7 subtract_bitcast_fusion
  1.4 0.6 select_reduce_fusion
  2.1 0.5 broadcast_add_fusion.pos
  2.6 0.0 copy-start
  2.6 193.0 %shard_map.37 = f32[2048,512]{1,0:T(8,128)} custom-call(s32[25]{0:T(128)} %get-tuple-element.6.ids, s32[25]{0:T(128)} %broadcast_add_fusion.pos, bf16[2048,4096]{1,0:T(8,128)(2,1)} %a_hbm.1, bf16[1,24,128,256]{3,2,1,0:T(8,128)(2,1)} %bitcast.10), custom_call_target="tpu_custom_call" | custom-call | tf_op jit(solution)/shard_map/pallas_call | solution.py:341
  195.6 0.0 copy-done
  195.6 0.2 compare_reduce_fusion
  195.8 0.1 broadcast_bitcast_fusion
  195.9 3.9 %select_bitcast_fusion = f32[1,2048,512]{2,1,0:T(8,128)} fusion(f32[2048,512]{1,0:T(8,128)} %shard_map.37, pred[2048]{0:T(1024)(128)(4,1)S(1)} %broadcast_bitcast_fusion), kind=kLoop, calls=%fused_computation | loop fusion | flops 2097152 | bytes 8390656 | tf_op jit(solution)/shard_map/broadcast_in_dim | solution.py:362
  (2 shorter events, 0.0 us)
Async XLA Ops:
  2.6 193.0 %copy-start = (s32[1,96]{1,0:T(1,128)S(1)}, s32[1,96]{1,0:T(1,128)}, u32[]{:S(2)}) copy-start(s32[1,96]{1,0:T(1,128)} %param.5) | copy-start | bytes 1156

commit v4 on v3

--- a/solution.py
+++ b/solution.py
@@ -220,23 +220,50 @@
         one = jnp.where(x < NX - 1 - x, x + (i - near), x - (i - near))
         return jnp.where(i <= 2 * near, two, one)
 
+    lead = jnp.where((z > 0) & (z + 1 < NZ), min(2, NZ - 1), 1)
+
+    def turn(s):
+        u = s - lead - 1
+        both = 2 * (NZ - 1 - lead)
+        own = (s <= lead) | ((u < both) & (u % 2 == 1))
+        zi = jnp.where(s <= lead, s, jnp.where(u < both, jnp.where(u % 2 == 1, lead + 1 + u // 2, u // 2), u - both // 2))
+        return zi, own
+
     def slice_at(s):
         if NX != 2:
             return zorder(s // NX) * NX + xorder(s % NX)
-        lead = jnp.where((z > 0) & (z + 1 < NZ), min(2, NZ - 1), 1)
-        u = s - lead - 1
-        both = 2 * (NZ - 1 - lead)
-        z_turn = (s <= lead) | ((u < both) & (u % 2 == 1))
-        zi = jnp.where(s <= lead, s, jnp.where(u < both, jnp.where(u % 2 == 1, lead + 1 + u // 2, u // 2), u - both // 2))
-        return zorder(zi) * NX + jnp.where(z_turn, x, 1 - x)
+        zi, own = turn(s)
+        return zorder(zi) * NX + jnp.where(own, x, 1 - x)
+
+    def pass_on(j, h, part):
+        e_copy(j, h, part, nbrs[0][1], 0).wait_recv()
+        forward(j, h, part, lambda cp: cp.start())
 
     def arrive(j, h):
-        for part in PARTS:
-            e_copy(j, h, part, nbrs[0][1], 0).wait_recv()
-            forward(j, h, part, lambda cp: cp.start())
+        if NX != 2:
+            pass_on(j, h, PARTS[0])
+        else:
+            @pl.when(j % NX == x)
+            def _():
+                pass_on(j, h, PARTS[0])
+        pass_on(j, h, PARTS[1])
+
+    def early(s):
+        if NX == 2:
+            zi, own = turn(s)
+            first = NZ - 1 - lead
+            end = jnp.where(own | (zi > first), zi, jnp.where(zi == first, NZ, zi + 1))
+
+            def one(i, carry):
+                for h in range(H):
+                    pass_on(zorder(i) * NX + 1 - x, h, PARTS[0])
+                return carry
+
+            lax.fori_loop(zi, end, one, 0)
 
     def step(s, carry):
         j, before = slice_at(s), slice_at(s - 1)
+        early(s)
         first_half(before, 0, w)
         for h in range(H):
             arrive(j, h)

time: 200 us -> 211 us (1.055)
  Pallas kernels: 193 us -> 204 us
    pallas_call x1, Pallas kernels: 193 us -> 204 us  [body(): pl.pallas_call(functools.partial(kernel, (NZ, NX, NC, CAP, H, MB, MM, KA)...]
where the time goes in v4:
time: 211 us
  Pallas kernels  204 us (97%)
  other arithmetic  6.67 us (3%)
    pallas_call x1, Pallas kernels, body(): pl.pallas_call(functools.partial(kernel, (NZ, NX, NC, CAP, H, MB, MM, KA)...  204 us

profile of v4, /device:TPU:7, one launch (start us, length us, event | category | flops | bytes accessed | tf_op | source)
XLA Modules:
  0.0 210.7 jit_solution(9192398153117976562)
XLA Ops:
  0.0 0.7 compare_bitcast_fusion
  0.7 0.1 convert_reduce_fusion
  0.8 0.7 subtract_bitcast_fusion
  1.4 0.6 select_reduce_fusion
  2.1 0.5 broadcast_add_fusion.pos
  2.6 0.0 copy-start
  2.6 203.9 %shard_map.37 = f32[2048,512]{1,0:T(8,128)} custom-call(s32[25]{0:T(128)} %get-tuple-element.6.ids, s32[25]{0:T(128)} %broadcast_add_fusion.pos, bf16[2048,4096]{1,0:T(8,128)(2,1)} %a_hbm.1, bf16[1,24,128,256]{3,2,1,0:T(8,128)(2,1)} %bitcast.10), custom_call_target="tpu_custom_call" | custom-call | tf_op jit(solution)/shard_map/pallas_call | solution.py:368
  206.6 0.0 copy-done
  206.6 0.2 compare_reduce_fusion
  206.8 0.1 broadcast_bitcast_fusion
  206.8 3.9 %select_bitcast_fusion = f32[1,2048,512]{2,1,0:T(8,128)} fusion(f32[2048,512]{1,0:T(8,128)} %shard_map.37, pred[2048]{0:T(1024)(128)(4,1)S(1)} %broadcast_bitcast_fusion), kind=kLoop, calls=%fused_computation | loop fusion | flops 2097152 | bytes 8390656 | tf_op jit(solution)/shard_map/broadcast_in_dim | solution.py:389
  (2 shorter events, 0.0 us)
Async XLA Ops:
  2.6 204.0 %copy-start = (s32[1,96]{1,0:T(1,128)S(1)}, s32[1,96]{1,0:T(1,128)}, u32[]{:S(2)}) copy-start(s32[1,96]{1,0:T(1,128)} %param.5) | copy-start | bytes 1156

commit v5 on v3

--- a/solution.py
+++ b/solution.py
@@ -89,7 +89,7 @@
 
     lax.fori_loop(0, NA_CH // 2, pack, 0)
 
-    PARTS = ((1, KA, K - KA), (0, 0, KA))
+    PARTS = ((0, 0, KA), (1, KA, K - KA))
 
     def e_copy(j, h, part, dev, d):
         p, first, count = part
@@ -106,7 +106,7 @@
                 along_x & (xs <= x) & (x + 1 < NX), along_x & (xs >= x) & (x > 0)]
 
     def forward(j, h, part, act):
-        for d in (2, 3, 0, 1):
+        for d in range(4):
             @pl.when(flags(j, part[0])[d])
             def _(d=d):
                 act(e_copy(j, h, part, nbrs[d][1], d))
@@ -315,7 +315,7 @@
     MM = min(512, HM)
     RB = 256
     K = CAP * BS
-    KA = (CAP - (CAP + 3) // 6) * BS
+    KA = (CAP - (CAP + 7) // 10) * BS
     s = structure[0]
     n = s.shape[0]
     at = jnp.arange(n, dtype=jnp.int32)

time: 200 us -> 199 us (level)
  no operation moved by 1% of the time
where the time goes in v5:
time: 199 us; the launch traced here: 198 us
  Pallas kernels  192 us (96%)
  other arithmetic  6.67 us (3%)
    pallas_call x1, Pallas kernels, body(): pl.pallas_call(functools.partial(kernel, (NZ, NX, NC, CAP, H, MB, MM, KA)...  192 us

profile of v5, /device:TPU:7, one launch (start us, length us, event | category | flops | bytes accessed | tf_op | source)
XLA Modules:
  0.0 198.3 jit_solution(17184481077342985991)
XLA Ops:
  0.0 0.7 compare_bitcast_fusion
  0.7 0.1 convert_reduce_fusion
  0.8 0.7 subtract_bitcast_fusion
  1.4 0.6 select_reduce_fusion
  2.1 0.5 broadcast_add_fusion.pos
  2.6 0.0 copy-start
  2.6 191.5 %shard_map.37 = f32[2048,512]{1,0:T(8,128)} custom-call(s32[25]{0:T(128)} %get-tuple-element.6.ids, s32[25]{0:T(128)} %broadcast_add_fusion.pos, bf16[2048,4096]{1,0:T(8,128)(2,1)} %a_hbm.1, bf16[1,24,128,256]{3,2,1,0:T(8,128)(2,1)} %bitcast.10), custom_call_target="tpu_custom_call" | custom-call | tf_op jit(solution)/shard_map/pallas_call | solution.py:341
  194.2 0.0 copy-done
  194.2 0.2 compare_reduce_fusion
  194.4 0.1 broadcast_bitcast_fusion
  194.4 3.9 %select_bitcast_fusion = f32[1,2048,512]{2,1,0:T(8,128)} fusion(f32[2048,512]{1,0:T(8,128)} %shard_map.37, pred[2048]{0:T(1024)(128)(4,1)S(1)} %broadcast_bitcast_fusion), kind=kLoop, calls=%fused_computation | loop fusion | flops 2097152 | bytes 8390656 | tf_op jit(solution)/shard_map/broadcast_in_dim | solution.py:362
  (2 shorter events, 0.0 us)
Async XLA Ops:
  2.6 191.6 %copy-start = (s32[1,96]{1,0:T(1,128)S(1)}, s32[1,96]{1,0:T(1,128)}, u32[]{:S(2)}) copy-start(s32[1,96]{1,0:T(1,128)} %param.5) | copy-start | bytes 1156

commit v6 on v5

--- a/solution.py
+++ b/solution.py
@@ -105,8 +105,8 @@
         return [along_z & (zs <= z) & (z + 1 < NZ), along_z & (zs >= z) & (z > 0),
                 along_x & (xs <= x) & (x + 1 < NX), along_x & (xs >= x) & (x > 0)]
 
-    def forward(j, h, part, act):
-        for d in range(4):
+    def forward(j, h, part, act, ways=range(4)):
+        for d in ways:
             @pl.when(flags(j, part[0])[d])
             def _(d=d):
                 act(e_copy(j, h, part, nbrs[d][1], d))
@@ -220,35 +220,54 @@
         one = jnp.where(x < NX - 1 - x, x + (i - near), x - (i - near))
         return jnp.where(i <= 2 * near, two, one)
 
+    lead = jnp.where((z > 0) & (z + 1 < NZ), min(2, NZ - 1), 1)
+
+    def turn(s):
+        u = s - lead - 1
+        both = 2 * (NZ - 1 - lead)
+        own = (s <= lead) | ((u < both) & (u % 2 == 1))
+        zi = jnp.where(s <= lead, s, jnp.where(u < both, jnp.where(u % 2 == 1, lead + 1 + u // 2, u // 2), u - both // 2))
+        return zi, own
+
     def slice_at(s):
         if NX != 2:
             return zorder(s // NX) * NX + xorder(s % NX)
-        lead = jnp.where((z > 0) & (z + 1 < NZ), min(2, NZ - 1), 1)
-        u = s - lead - 1
-        both = 2 * (NZ - 1 - lead)
-        z_turn = (s <= lead) | ((u < both) & (u % 2 == 1))
-        zi = jnp.where(s <= lead, s, jnp.where(u < both, jnp.where(u % 2 == 1, lead + 1 + u // 2, u // 2), u - both // 2))
-        return zorder(zi) * NX + jnp.where(z_turn, x, 1 - x)
-
-    def arrive(j, h):
+        zi, own = turn(s)
+        return zorder(zi) * NX + jnp.where(own, x, 1 - x)
+
+    def start(cp):
+        cp.start()
+
+    def arrive(s, h):
+        j = slice_at(s)
         for part in PARTS:
             e_copy(j, h, part, nbrs[0][1], 0).wait_recv()
-            forward(j, h, part, lambda cp: cp.start())
+            if NX != 2:
+                forward(j, h, part, start)
+                continue
+            forward(j, h, part, start, (0, 1))
+            if part[0] == 0:
+                zi, own = turn(s)
+
+                @pl.when(jnp.logical_not(own) & (zi + 1 < NZ))
+                def _():
+                    forward(zorder(zi + 1) * NX + x, h, part, start, (2, 3))
 
     def step(s, carry):
-        j, before = slice_at(s), slice_at(s - 1)
+        before = slice_at(s - 1)
         first_half(before, 0, w)
         for h in range(H):
-            arrive(j, h)
+            arrive(s, h)
             if h == 0:
                 second_half(before, 0, w)
         return carry
 
     lax.fori_loop(1, NR - 1, step, 0)
-    last, before = slice_at(jnp.int32(NR - 1)), slice_at(jnp.int32(NR - 2))
+    end = jnp.int32(NR - 1)
+    last, before = slice_at(end), slice_at(end - 1)
     first_half(before, 0, w)
     for h in range(H):
-        arrive(last, h)
+        arrive(end, h)
         if h == 0:
             second_half(before, 0, w)
         first_half(last, h * wh, wh)

time: 199 us -> 206 us (1.035)
  Pallas kernels: 192 us -> 199 us
    pallas_call x1, Pallas kernels: 192 us -> 199 us  [body(): pl.pallas_call(functools.partial(kernel, (NZ, NX, NC, CAP, H, MB, MM, KA)...]
where the time goes in v6:
time: 206 us; the launch traced here: 205 us
  Pallas kernels  199 us (97%)
  other arithmetic  6.67 us (3%)
    pallas_call x1, Pallas kernels, body(): pl.pallas_call(functools.partial(kernel, (NZ, NX, NC, CAP, H, MB, MM, KA)...  199 us

profile of v6, /device:TPU:7, one launch (start us, length us, event | category | flops | bytes accessed | tf_op | source)
XLA Modules:
  0.0 205.3 jit_solution(2166986595937986116)
XLA Ops:
  0.0 0.7 compare_bitcast_fusion
  0.7 0.1 convert_reduce_fusion
  0.8 0.7 subtract_bitcast_fusion
  1.4 0.6 select_reduce_fusion
  2.1 0.5 broadcast_add_fusion.pos
  2.6 0.0 copy-start
  2.6 198.5 %shard_map.37 = f32[2048,512]{1,0:T(8,128)} custom-call(s32[25]{0:T(128)} %get-tuple-element.6.ids, s32[25]{0:T(128)} %broadcast_add_fusion.pos, bf16[2048,4096]{1,0:T(8,128)(2,1)} %a_hbm.1, bf16[1,24,128,256]{3,2,1,0:T(8,128)(2,1)} %bitcast.10), custom_call_target="tpu_custom_call" | custom-call | tf_op jit(solution)/shard_map/pallas_call | solution.py:360
  201.2 0.0 copy-done
  201.2 0.2 compare_reduce_fusion
  201.4 0.1 broadcast_bitcast_fusion
  201.4 3.9 %select_bitcast_fusion = f32[1,2048,512]{2,1,0:T(8,128)} fusion(f32[2048,512]{1,0:T(8,128)} %shard_map.37, pred[2048]{0:T(1024)(128)(4,1)S(1)} %broadcast_bitcast_fusion), kind=kLoop, calls=%fused_computation | loop fusion | flops 2097152 | bytes 8390656 | tf_op jit(solution)/shard_map/broadcast_in_dim | solution.py:381
  (2 shorter events, 0.0 us)
Async XLA Ops:
  2.6 198.6 %copy-start = (s32[1,96]{1,0:T(1,128)S(1)}, s32[1,96]{1,0:T(1,128)}, u32[]{:S(2)}) copy-start(s32[1,96]{1,0:T(1,128)} %param.5) | copy-start | bytes 1156

commit v7 on v2

--- a/solution.py
+++ b/solution.py
@@ -106,7 +106,7 @@
                 along_x & (xs <= x) & (x + 1 < NX), along_x & (xs >= x) & (x > 0)]
 
     def forward(j, h, part, act):
-        for d in (2, 3, 0, 1):
+        for d in range(4):
             @pl.when(flags(j, part[0])[d])
             def _(d=d):
                 act(e_copy(j, h, part, nbrs[d][1], d))
@@ -300,7 +300,7 @@
     MM = min(512, HM)
     RB = 256
     K = CAP * BS
-    KA = (CAP - (CAP + 3) // 6) * BS
+    KA = (CAP - (CAP + 7) // 10) * BS
     s = structure[0]
     n = s.shape[0]
     at = jnp.arange(n, dtype=jnp.int32)

time: 197 us -> 196 us (level)
  no operation moved by 1% of the time
where the time goes in v7:
time: 196 us
  Pallas kernels  189 us (96%)
  other arithmetic  6.67 us (3%)
    pallas_call x1, Pallas kernels, body(): pl.pallas_call(functools.partial(kernel, (NZ, NX, NC, CAP, H, MB, MM, KA)...  189 us

profile of v7, /device:TPU:7, one launch (start us, length us, event | category | flops | bytes accessed | tf_op | source)
XLA Modules:
  0.0 195.8 jit_solution(9038176149626366068)
XLA Ops:
  0.0 0.7 compare_bitcast_fusion
  0.7 0.1 convert_reduce_fusion
  0.8 0.7 subtract_bitcast_fusion
  1.4 0.6 select_reduce_fusion
  2.1 0.5 broadcast_add_fusion.pos
  2.6 0.0 copy-start
  2.6 189.0 %shard_map.37 = f32[2048,512]{1,0:T(8,128)} custom-call(s32[25]{0:T(128)} %get-tuple-element.6.ids, s32[25]{0:T(128)} %broadcast_add_fusion.pos, bf16[2048,4096]{1,0:T(8,128)(2,1)} %a_hbm.1, bf16[1,24,128,256]{3,2,1,0:T(8,128)(2,1)} %bitcast.10), custom_call_target="tpu_custom_call" | custom-call | tf_op jit(solution)/shard_map/pallas_call | solution.py:326
  191.7 0.0 copy-done
  191.7 0.2 compare_reduce_fusion
  191.9 0.1 broadcast_bitcast_fusion
  191.9 3.9 %select_bitcast_fusion = f32[1,2048,512]{2,1,0:T(8,128)} fusion(f32[2048,512]{1,0:T(8,128)} %shard_map.37, pred[2048]{0:T(1024)(128)(4,1)S(1)} %broadcast_bitcast_fusion), kind=kLoop, calls=%fused_computation | loop fusion | flops 2097152 | bytes 8390656 | tf_op jit(solution)/shard_map/broadcast_in_dim | solution.py:347
  (2 shorter events, 0.0 us)
Async XLA Ops:
  2.6 189.1 %copy-start = (s32[1,96]{1,0:T(1,128)S(1)}, s32[1,96]{1,0:T(1,128)}, u32[]{:S(2)}) copy-start(s32[1,96]{1,0:T(1,128)} %param.5) | copy-start | bytes 1156
